TPU v7x, 32 devices: a whole 2x2x4 slice. The times are simulated.
32 devices in a mesh: seq: 8 (over z, y), chan: 4 (over x, core).
Axes of the slice: x: 2, y: 2, z: 4, core: 2. Of those that a mesh axis runs over, the one named last changes fastest.
Arguments:
- inputs: bfloat16 [1024, 4096], P('seq', 'chan'), may hold values from -6 to 6
- grads: bfloat16 [1024, 4096], P('seq', 'chan'), may hold values from -0.5 to 0.5
- filter_taps: float32 [256, 4096], P(('seq', 'chan')), may hold values from -6 to 6
- supports: int32 [32], replicated, may hold values from 1 to 2, as said below
Outputs:
- grad_inputs: bfloat16 [1024, 4096], P('seq', 'chan')
- grad_filter: float32 [256, 4096], P(('seq', 'chan'))
Inputs may be any that keep to these rules, and one draw needn't show every extreme that they name: `supports`: some group spans 2 blocks and some group spans 1 block.
All inputs are finite; a program needn't handle non-finite values.
Results may differ from a plain program's by a relative error of at most 0.001.
Values may be sent and summed in bfloat16 or wider, within the bound.
No kernel may reach another device: no remote copies, remote signals or barrier semaphores. Data moves between devices by JAX's collectives and lax.ppermute only.
A program may use at most 64 MiB of HBM per device.

v0:
```python
import math

import jax
import jax.numpy as jnp
from jax import lax
from jax.sharding import PartitionSpec as P

GROUP_CH = 128


HIGHEST = lax.Precision.HIGHEST


def passed_along(value, axis, by):
    length = lax.axis_size(axis)
    pairs = [(i, i + by) for i in range(length) if 0 <= i + by < length]
    return lax.ppermute(value, axis, pairs)


def fourier_tables(span_len, block_len):
    index = jnp.arange(span_len, dtype=jnp.int32)
    phase = index[:, None] * index[None, :] % span_len
    angles = phase.astype(jnp.float32) * (2.0 * math.pi / span_len)
    cosine = jnp.cos(angles)
    sine = jnp.sin(angles)
    forward_full = jnp.concatenate([cosine, -sine], axis=0)
    forward_half = forward_full[:, :block_len]
    inverse = jnp.concatenate([cosine, -sine], axis=1) / span_len
    return (forward_full, forward_half, inverse)


def apply_table(table, values):
    return jnp.dot(table, values, precision=HIGHEST, preferred_element_type=jnp.float32)


def times_conj(first, second, half):
    first_re, first_im = (first[:half], first[half:])
    second_re, second_im = (second[:half], second[half:])
    real_part = first_re * second_re + first_im * second_im
    imag_part = first_im * second_re - first_re * second_im
    return jnp.concatenate([real_part, imag_part], axis=0)


def body(inputs, grads, filter_taps, supports):
    block_len, width_here = inputs.shape
    span_len = 2 * block_len
    chan_index = lax.axis_index("chan")
    seq_count = lax.axis_size("seq")
    reach = max(2, seq_count // 16)
    lag_total = reach * block_len
    groups_here = width_here // GROUP_CH
    own_support = lax.dynamic_slice_in_dim(supports, chan_index * groups_here, groups_here, 0)
    limit = jnp.repeat(own_support, GROUP_CH) * block_len
    lag_pos = jnp.arange(lag_total, dtype=jnp.int32)[:, None]
    own_taps = lax.all_to_all(filter_taps, "chan", split_axis=1, concat_axis=0, tiled=True)
    all_taps = lax.all_gather(own_taps, "seq", axis=0, tiled=True)
    all_taps = jnp.where(lag_pos < limit[None, :], all_taps, 0.0)
    padded_taps = jnp.pad(all_taps, ((block_len, block_len), (0, 0)))
    forward_full, forward_half, inverse = fourier_tables(span_len, block_len)
    own_grad_spec = apply_table(forward_half, grads.astype(jnp.float32))
    window_list = []
    for offset in range(reach + 1):
        window = padded_taps[offset * block_len : offset * block_len + span_len]
        circular = jnp.concatenate([window[block_len:], window[:block_len]], axis=0)
        window_list.append(apply_table(forward_full, circular))
    window_specs = jnp.stack(window_list, axis=0)

    def pair_update(step, signal_blk, upstream_blk, lag_sums, input_spec):
        signal_spec = apply_table(forward_half, signal_blk.astype(jnp.float32))
        upstream_spec = apply_table(forward_half, upstream_blk.astype(jnp.float32))
        window_spec = lax.dynamic_index_in_dim(window_specs, step, 0, keepdims=False)
        corr = apply_table(inverse, times_conj(own_grad_spec, signal_spec, span_len))
        shifted = jnp.concatenate([corr[block_len:], corr[:block_len]], axis=0)
        current = lax.dynamic_slice_in_dim(lag_sums, step * block_len, span_len, 0)
        lag_sums = lax.dynamic_update_slice_in_dim(lag_sums, current + shifted, step * block_len, 0)
        input_spec = input_spec + times_conj(upstream_spec, window_spec, span_len)
        return (lag_sums, input_spec)

    lag_sums = jnp.zeros(((reach + 2) * block_len, width_here), jnp.float32)
    input_spec = jnp.zeros((2 * span_len, width_here), jnp.float32)
    lag_sums, input_spec = pair_update(0, inputs, grads, lag_sums, input_spec)

    def passed_step(step, carry):
        signal_now, upstream_now, sums_now, spec_now = carry
        signal_now = passed_along(signal_now, "seq", 1)
        upstream_now = passed_along(upstream_now, "seq", -1)
        sums_now, spec_now = pair_update(step, signal_now, upstream_now, sums_now, spec_now)
        return (signal_now, upstream_now, sums_now, spec_now)

    carried = lax.fori_loop(1, reach + 1, passed_step, (inputs, grads, lag_sums, input_spec))
    lag_sums, input_spec = (carried[2], carried[3])
    grad_inputs = apply_table(inverse[:block_len], input_spec).astype(jnp.bfloat16)
    filter_term = lag_sums[block_len : block_len + lag_total]
    filter_term = jnp.where(lag_pos < limit[None, :], filter_term, 0.0)
    owned = lax.psum_scatter(filter_term, "seq", scatter_dimension=0, tiled=True)
    grad_filter = lax.all_to_all(owned, "chan", split_axis=0, concat_axis=1, tiled=True)
    return (grad_inputs, grad_filter)


def solution(mesh):
    in_specs = (P("seq", "chan"), P("seq", "chan"), P(("seq", "chan"), None), P())
    out_specs = (P("seq", "chan"), P(("seq", "chan"), None))
    return jax.shard_map(body, mesh=mesh, in_specs=in_specs, out_specs=out_specs, check_vma=False)
```

profile of v0, /device:TPU:0, one launch (start us, length us, event | category | flops | bytes accessed | tf_op | source)
XLA Modules:
  0.0 206.3 jit_solution(3756340968511003766)
XLA Ops:
  7.2 1.7 copy.25
  8.9 1.7 copy.26
  10.5 9.4 %all_to_all.38 = f32[8,4,1024]{2,0,1:T(8,128)} all-to-all(f32[8,4,1024]{2,0,1:T(8,128)} %bitcast.70), channel_id=1, replica_groups=mesh['seq'=8,'chan'=4] {'chan'}, dimensions={1} | all-to-all | bytes 262144 | tf_op jit(solution)/shard_map/all_to_all | solution.py:55
  23.0 3.2 %fusion.41 = f32[512,1024]{1,0:T(8,128)} fusion(f32[512,128]{1,0:T(8,128)S(1)} %pad_maximum_fusion.6, bf16[128,1024]{1,0:T(8,128)(2,1)} %copy.25), kind=kOutput, calls=%fused_computation.72 | convolution fusion | flops 805306368 | bytes 2621440 | tf_op jit(solution)/shard_map/dot_general | solution.py:33
  26.2 35.1 %all-gather.2.cloned.1.call-done = f32[256,1024]{1,0:T(8,128)} async-done(((f32[32,1024]{1,0:T(8,128)}), f32[256,1024]{1,0:T(8,128)}) %all-gather.2.cloned.1.call-update) | async-done | bytes 1048592 | tf_op jit(solution)/shard_map/all_gather | solution.py:56
  62.8 2.0 convolution_bitcast_fusion.2
  64.8 1.8 convolution_bitcast_fusion
  66.6 1.9 convolution_bitcast_fusion.1
  69.2 1.9 fusion.9
  71.3 3.2 %pad_maximum_fusion = f32[3,512,1024]{2,1,0:T(8,128)} fusion(f32[1,512,1024]{2,1,0:T(8,128)S(1)} %convolution_bitcast_fusion, f32[1,512,1024]{2,1,0:T(8,128)S(1)} %convolution_bitcast_fusion.1, f32[1,512,1024]{2,1,0:T(8,128)S(1)} %convolution_bitcast_fusion.2), kind=kLoop, calls=%fused_computation.15 | loop fusion | flops 3145728 | bytes 12582912 | tf_op jit(solution)/shard_map/stack | solution.py:66
  77.7 46.8 %while.21 = (s32[]{:T(128)}, bf16[128,1024]{1,0:T(8,128)(2,1)}, bf16[128,1024]{1,0:T(8,128)(2,1)}, f32[512,1024]{1,0:T(8,128)}, f32[512,1024]{1,0:T(8,128)}, /*i...) while((s32[]{:T(128)}, bf16[128,1024]{1,0:T(8,128)(2,1)}, ...), condition=%wide.region_1.2_spmd, body=%wide.region_0.1_spmd.sunk | while | flops 3226468352 | bytes 69730744 | solution.py:90
  77.7 2.5 %collective-permute-start = (bf16[128,1024]{1,0:T(8,128)(2,1)}, bf16[128,1024]{1,0:T(8,128)(2,1)S(1)}, u32[]{:S(2)}, u32[]{:S(2)}) collective-permute-start(bf16[128,1024]{1,0:T(8,128)(2,1)} %get-tuple-element.344), channel_id=1, source_target_pairs={{0,4},{4,8},{8,12},{12,16},{16,20},{20,24},{24,28},{1,5},{5,9},{9,... | collective-permute-start | bytes 786440 | tf_op jit(solution)/shard_map/while/body/eval_jaxpr/ppermute | solution.py:17
  81.5 8.7 %collective-permute-done = bf16[128,1024]{1,0:T(8,128)(2,1)S(1)} collective-permute-done((bf16[128,1024]{1,0:T(8,128)(2,1)}, bf16[128,1024]{1,0:T(8,128)(2,1)S(1)}, u32[]{:S(2)}, u32[]{:S(2)}) %collective-permute-start) | collective-permute-done | bytes 262176 | tf_op jit(solution)/shard_map/while/body/eval_jaxpr/ppermute | solution.py:17
  91.6 2.0 fusion.70
  94.7 2.1 %multiply_add_fusion.7 = (f32[256,1024]{1,0:T(8,128)S(1)}, f32[256,1024]{1,0:T(8,128)S(1)}) fusion(f32[512,1024]{1,0:T(8,128)S(1)} %fusion.73, f32[3,512,1024]{2,1,0:T(8,128)} %get-tuple-element.366, s32[]{:T(128)S(6)} %select_n.64, s32[]{:T(128)S(6)} %add.150), kind=kLoop, calls=%fused_computation.11.clone.1 | loop fusion | flops 1572864 | bytes 6291464 | tf_op jit(solution)/shard_map/while/body/eval_jaxpr/add | solution.py:39
  100.3 4.3 %collective-permute-start = (bf16[128,1024]{1,0:T(8,128)(2,1)}, bf16[128,1024]{1,0:T(8,128)(2,1)S(1)}, u32[]{:S(2)}, u32[]{:S(2)}) collective-permute-start(bf16[128,1024]{1,0:T(8,128)(2,1)} %get-tuple-element.344), channel_id=1, source_target_pairs={{0,4},{4,8},{8,12},{12,16},{16,20},{20,24},{24,28},{1,5},{5,9},{9,... | collective-permute-start | bytes 786440 | tf_op jit(solution)/shard_map/while/body/eval_jaxpr/ppermute | solution.py:17
  105.9 8.5 %collective-permute-done = bf16[128,1024]{1,0:T(8,128)(2,1)S(1)} collective-permute-done((bf16[128,1024]{1,0:T(8,128)(2,1)}, bf16[128,1024]{1,0:T(8,128)(2,1)S(1)}, u32[]{:S(2)}, u32[]{:S(2)}) %collective-permute-start) | collective-permute-done | bytes 262176 | tf_op jit(solution)/shard_map/while/body/eval_jaxpr/ppermute | solution.py:17
  115.8 2.0 fusion.70
  118.9 2.1 %multiply_add_fusion.7 = (f32[256,1024]{1,0:T(8,128)S(1)}, f32[256,1024]{1,0:T(8,128)S(1)}) fusion(f32[512,1024]{1,0:T(8,128)S(1)} %fusion.73, f32[3,512,1024]{2,1,0:T(8,128)} %get-tuple-element.366, s32[]{:T(128)S(6)} %select_n.64, s32[]{:T(128)S(6)} %add.150), kind=kLoop, calls=%fused_computation.11.clone.1 | loop fusion | flops 1572864 | bytes 6291464 | tf_op jit(solution)/shard_map/while/body/eval_jaxpr/add | solution.py:39
  124.5 2.5 %slice_select_fusion = f32[256,1024]{1,0:T(8,128)} fusion(f32[512,1024]{1,0:T(8,128)} %get-tuple-element.224, s32[1024]{0:T(1024)S(1)} %broadcast_bitcast_fusion), kind=kLoop, calls=%fused_computation.32 | loop fusion | flops 524288 | bytes 2101248 | tf_op jit(solution)/shard_map/jit(_where)/select_n | solution.py:94
  127.0 63.8 %reduce-scatter.2.cloned.1.call-done = f32[32,1024]{1,0:T(8,128)} async-done(((f32[256,1024]{1,0:T(8,128)}), f32[32,1024]{1,0:T(8,128)}) %reduce-scatter.2.cloned.1.call-update) | async-done | bytes 131088 | tf_op jit(solution)/shard_map/reduce_scatter | solution.py:95
  190.9 3.3 %all-to-all-start.1 = ((f32[4,8,1024]{2,1,0:T(8,128)}), f32[4,8,1024]{2,1,0:T(8,128)S(1)}, u32[]{:S(2)}, u32[]{:S(2)}) async-start(f32[4,8,1024]{2,1,0:T(8,128)} %bitcast.71), calls=%async_computation.2 | async-start | bytes 262144 | tf_op jit(solution)/shard_map/all_to_all | solution.py:96
  194.2 2.0 convolution_convert_fusion
  196.2 2.6 %all-to-all-done.1 = f32[4,8,1024]{2,1,0:T(8,128)S(1)} async-done(((f32[4,8,1024]{2,1,0:T(8,128)}), f32[4,8,1024]{2,1,0:T(8,128)S(1)}, u32[]{:S(2)}, u32[]{:S(2)}) %all-to-all-start.1) | async-done | bytes 131104 | tf_op jit(solution)/shard_map/all_to_all | solution.py:96
  (61 shorter events, 23.5 us)
Async XLA Ops:
  7.2 54.2 %all-gather.2.cloned.1.call-start = ((), (), s32[]{:S(2)}) async-start(), calls=%async_computation.3 | async-start | bytes 1179648 | tf_op jit(solution)/shard_map/all_gather | solution.py:56
  20.0 170.9 %reduce-scatter.2.cloned.1.call-start = ((), (), s32[]{:S(2)}) async-start(), calls=%async_computation.4 | async-start | bytes 1179648 | tf_op jit(solution)/shard_map/reduce_scatter | solution.py:95
  20.0 2.0 copy-start.6
  26.2 36.5 %copy-start.7 = (pred[256]{0:T(512)(128)(4,1)S(1)}, pred[256]{0:T(512)(128)(4,1)}, u32[]{:S(2)}) copy-start(pred[256]{0:T(512)(128)(4,1)} %constant.92.clone.1) | copy-start | bytes 772
  66.6 1.9 copy-start.5
  77.7 12.5 %collective-permute-start = (bf16[128,1024]{1,0:T(8,128)(2,1)}, bf16[128,1024]{1,0:T(8,128)(2,1)S(1)}, u32[]{:S(2)}, u32[]{:S(2)}) collective-permute-start(bf16[128,1024]{1,0:T(8,128)(2,1)} %get-tuple-element.344), channel_id=1, source_target_pairs={{0,4},{4,8},{8,12},{12,16},{16,20},{20,24},{24,28},{1,5},{5,9},{9,... | collective-permute-start | bytes 786440 | tf_op jit(solution)/shard_map/while/body/eval_jaxpr/ppermute | solution.py:17
  80.2 13.6 %collective-permute-start.1 = (bf16[128,1024]{1,0:T(8,128)(2,1)}, bf16[128,1024]{1,0:T(8,128)(2,1)S(1)}, u32[]{:S(2)}, u32[]{:S(2)}) collective-permute-start(bf16[128,1024]{1,0:T(8,128)(2,1)} %get-tuple-element.345), channel_id=1, source_target_pairs={{4,0},{8,4},{12,8},{16,12},{20,16},{24,20},{28,24},{5,1},{9,5},{13... | collective-permute-start | bytes 786440 | tf_op jit(solution)/shard_map/while/body/eval_jaxpr/ppermute | solution.py:17
  94.7 2.2 %copy-start = (f32[512,1024]{1,0:T(8,128)S(1)}, f32[512,1024]{1,0:T(8,128)}, u32[]{:S(2)}) copy-start(f32[512,1024]{1,0:T(8,128)} %get-tuple-element.347) | copy-start | bytes 6291460 | tf_op jit(solution)/shard_map/while
  97.0 1.6 copy-start.3
  97.6 2.7 %copy-start.1 = (f32[512,1024]{1,0:T(8,128)}, f32[512,1024]{1,0:T(8,128)S(1)}, u32[]{:S(2)}) copy-start(f32[512,1024]{1,0:T(8,128)S(1)} %maximum_add_fusion.3) | copy-start | bytes 6291460 | tf_op jit(solution)/shard_map/while
  98.8 1.5 copy-start.4
  100.3 14.1 %collective-permute-start = (bf16[128,1024]{1,0:T(8,128)(2,1)}, bf16[128,1024]{1,0:T(8,128)(2,1)S(1)}, u32[]{:S(2)}, u32[]{:S(2)}) collective-permute-start(bf16[128,1024]{1,0:T(8,128)(2,1)} %get-tuple-element.344), channel_id=1, source_target_pairs={{0,4},{4,8},{8,12},{12,16},{16,20},{20,24},{24,28},{1,5},{5,9},{9,... | collective-permute-start | bytes 786440 | tf_op jit(solution)/shard_map/while/body/eval_jaxpr/ppermute | solution.py:17
  104.6 13.3 %collective-permute-start.1 = (bf16[128,1024]{1,0:T(8,128)(2,1)}, bf16[128,1024]{1,0:T(8,128)(2,1)S(1)}, u32[]{:S(2)}, u32[]{:S(2)}) collective-permute-start(bf16[128,1024]{1,0:T(8,128)(2,1)} %get-tuple-element.345), channel_id=1, source_target_pairs={{4,0},{8,4},{12,8},{16,12},{20,16},{24,20},{28,24},{5,1},{9,5},{13... | collective-permute-start | bytes 786440 | tf_op jit(solution)/shard_map/while/body/eval_jaxpr/ppermute | solution.py:17
  118.9 2.2 %copy-start = (f32[512,1024]{1,0:T(8,128)S(1)}, f32[512,1024]{1,0:T(8,128)}, u32[]{:S(2)}) copy-start(f32[512,1024]{1,0:T(8,128)} %get-tuple-element.347) | copy-start | bytes 6291460 | tf_op jit(solution)/shard_map/while
  121.1 1.6 copy-start.3
  121.8 2.7 %copy-start.1 = (f32[512,1024]{1,0:T(8,128)}, f32[512,1024]{1,0:T(8,128)S(1)}, u32[]{:S(2)}) copy-start(f32[512,1024]{1,0:T(8,128)S(1)} %maximum_add_fusion.3) | copy-start | bytes 6291460 | tf_op jit(solution)/shard_map/while
  122.9 1.5 copy-start.4
  124.5 69.7 %copy-start.2 = (f32[512,1024]{1,0:T(8,128)S(1)}, f32[512,1024]{1,0:T(8,128)}, u32[]{:S(2)}) copy-start(f32[512,1024]{1,0:T(8,128)} %get-tuple-element.223) | copy-start | bytes 6291460
  190.9 7.9 %all-to-all-start.1 = ((f32[4,8,1024]{2,1,0:T(8,128)}), f32[4,8,1024]{2,1,0:T(8,128)S(1)}, u32[]{:S(2)}, u32[]{:S(2)}) async-start(f32[4,8,1024]{2,1,0:T(8,128)} %bitcast.71), calls=%async_computation.2 | async-start | bytes 262144 | tf_op jit(solution)/shard_map/all_to_all | solution.py:96
Sparse Core Ops, SparseCore 0:
  20.1 41.2 all-gather.1
  127.1 63.6 reduce-scatter.1
where the time goes:
time: 207 us; the launch traced here: 206 us
  waiting for transfers between devices  119 us (57%)
  matrix products  21.7 us (10%)
  other arithmetic  19.8 us (10%)
  between operations  14.2 us (7%)
  starting transfers between devices  12.7 us (6%)
  local copies, waits for them, and re-layouts  9.5 us (5%)
  blocking collectives  9.4 us (5%)
    reduce_scatter x1, waiting for transfers between devices, body(): lax.psum_scatter(filter_term, 'seq', scatter_dimension=0, tiled=True)  63.8 us
    all_gather x1, waiting for transfers between devices, body(): all_taps = lax.all_gather(own_taps, 'seq', axis=0, tiled=True)  35.1 us
    dot_general x13, matrix products, apply_table(): jnp.dot(table, values, precision=HIGHEST, preferred_element_type=jnp.floa...  21.7 us
    ppermute x4, waiting for transfers between devices, passed_along(): return lax.ppermute(value, axis, pairs)  17.2 us
    all_to_all x1, blocking collectives, body(): lax.all_to_all(filter_taps, 'chan', split_axis=1, concat_axis=0, tiled=True)  9.4 us
    ppermute x4, starting transfers between devices, passed_along(): return lax.ppermute(value, axis, pairs)  9.33 us
    add x5, other arithmetic, times_conj(): real_part = first_re * second_re + first_im * second_im  5.87 us
    while x20, local copies, waits for them, and re-layouts  5.03 us
  transfers between devices with their start and end apart: 7, of which 5 were waited for; matrix products, arithmetic and copies ran while one was open for 7% of the time, Pallas kernels for 0%

commit v1 on v0

v1 whole, which is shorter than its diff:
```python
import functools

import numpy as np
import ml_dtypes
import jax
import jax.numpy as jnp
from jax import lax
from jax.experimental import pallas as pl
from jax.experimental.pallas import tpu as pltpu
from jax.sharding import PartitionSpec as P

GROUP_CH = 128
LANES = 128
BF16 = jnp.bfloat16
F32 = jnp.float32
EVERY = ("seq", "chan")
VMEM = pl.BlockSpec(memory_space=pltpu.VMEM)
HBM = pl.BlockSpec(memory_space=pltpu.HBM)
SMEM = pl.BlockSpec(memory_space=pltpu.SMEM)
PARAMS = pltpu.CompilerParams(vmem_limit_bytes=40 * 1024 * 1024)


def split_table(table):
    high = table.astype(ml_dtypes.bfloat16)
    low = (table - high.astype(np.float64)).astype(ml_dtypes.bfloat16)
    return high, low


def tables(lags):
    freqs = np.concatenate([np.arange(0, lags, 2), np.arange(1, lags, 2)]) + 0.5
    angle = freqs[:, None] * np.arange(lags)[None, :] * (np.pi / lags)
    forward = np.concatenate([np.cos(angle), -np.sin(angle)], axis=0)
    parts = split_table(forward) + split_table(forward.T / lags)
    return [jnp.asarray(part) for part in parts]


def split_values(values):
    high = values.astype(BF16)
    return high, (values - high.astype(F32)).astype(BF16)


def split_outside(values):
    high = lax.reduce_precision(values, 8, 7)
    return [high.astype(BF16), (values - high).astype(BF16)]


def dot(first, second):
    return jnp.dot(first, second, preferred_element_type=F32)


def dot_exact(table, values):
    return dot(table[0], values) + dot(table[1], values)


def dot_split(table, values):
    high, low = split_values(values)
    return dot(table[0], high) + (dot(table[0], low) + dot(table[1], high))


def conj_product(first, second, half):
    first_re, first_im = first[:half], first[half:]
    second_re, second_im = second[:half], second[half:]
    return jnp.concatenate(
        [first_re * second_re + first_im * second_im, first_im * second_re - first_re * second_im], axis=0
    )


def add_next(own, following, lags):
    quarter = lags // 2
    parts = [own[i * quarter : (i + 1) * quarter] for i in range(4)]
    nexts = [following[i * quarter : (i + 1) * quarter] for i in range(4)]
    return jnp.concatenate(
        [parts[0] + nexts[2], parts[1] - nexts[3], parts[2] - nexts[0], parts[3] + nexts[1]], axis=0
    )


def conv_grads(lags, upstream, signal, taps, limit, forward, inverse):
    blocks, width = len(upstream), upstream[0].shape[1]
    if width == LANES:
        joined = dot_exact(forward, jnp.concatenate(upstream + signal + taps, axis=1))
        specs = [joined[:, k * width : (k + 1) * width] for k in range(2 * blocks + 2)]
    else:
        specs = [dot_exact(forward, part) for part in upstream + signal + taps]
    taps_spec = specs[2 * blocks] + specs[2 * blocks + 1]
    products, filter_spec = [], None
    for k in range(blocks):
        window = add_next(specs[k], specs[k + 1], lags) if k + 1 < blocks else specs[k]
        products.append(conj_product(window, taps_spec, lags))
        term = conj_product(window, specs[blocks + k], lags)
        filter_spec = term if filter_spec is None else filter_spec + term
    products.append(filter_spec)
    if width == LANES:
        joined = dot_split(inverse, jnp.concatenate(products, axis=1))
        results = [joined[:, k * width : (k + 1) * width] for k in range(blocks + 1)]
    else:
        results = [dot_split(inverse, product) for product in products]
    lag_pos = lax.broadcasted_iota(jnp.int32, results[-1].shape, 0)
    return results[:-1], jnp.where(lag_pos < limit, results[-1], 0.0)


def swap_table():
    quarter = LANES // 4
    index = np.arange(4 * LANES)
    part, block, lane = index // LANES, index % LANES // quarter, index % quarter
    target = block * LANES + part * quarter + lane
    table = np.zeros((4 * LANES, 4 * LANES), ml_dtypes.bfloat16)
    table[index, target] = 1
    return jnp.asarray(table)


def swap_blocks(stacks, table):
    rows = stacks[0][0].shape[0]
    side = [jnp.concatenate(parts, axis=1) for parts in stacks]
    moved = dot(jnp.concatenate(side, axis=0), table).astype(BF16)
    return [
        [moved[i * rows : (i + 1) * rows, l * LANES : (l + 1) * LANES] for l in range(4)] for i in range(len(stacks))
    ]


def split_rows(values):
    high = values.astype(BF16).astype(F32)
    return jnp.concatenate([high, values - high], axis=0).astype(BF16)


def pack_kernel(grad_hbm, signal_hbm, taps_hbm, table_hbm, out_ref, grad_ref, signal_ref, taps_ref, table_ref, sems):
    pairs = ((table_hbm, table_ref), (grad_hbm, grad_ref), (signal_hbm, signal_ref), (taps_hbm, taps_ref))
    copies = [pltpu.make_async_copy(source, target, sems.at[i]) for i, (source, target) in enumerate(pairs)]
    for copy in copies:
        copy.start()
    rows, width_here = grad_ref.shape
    piece = rows // 4
    tiles = range(width_here // LANES)
    copies[0].wait()
    table = table_ref[...]
    for at, source, copy in ((0, grad_ref, copies[1]), (piece, signal_ref, copies[2])):
        copy.wait()
        moved = swap_blocks(
            [
                [source[q * piece : (q + 1) * piece, tile * LANES : (tile + 1) * LANES] for q in range(4)]
                for tile in tiles
            ],
            table,
        )
        for tile in tiles:
            for l in range(4):
                out_ref[tile * 4 + l, at : at + piece, :] = moved[tile][l]
    copies[3].wait()
    starts = [[c * width_here + tile * LANES for c in range(4)] for tile in tiles]
    moved = swap_blocks([[split_rows(taps_ref[:, at : at + LANES]) for at in row] for row in starts], table)
    for tile in tiles:
        for l in range(4):
            out_ref[tile * 4 + l, 2 * piece :, :] = moved[tile][l]


def lane_limit(support_ref, width):
    lane = lax.broadcasted_iota(jnp.int32, (1, width), 1)
    parts = support_ref.shape[0]
    limit = jnp.zeros((1, width), jnp.int32)
    for part in range(parts):
        limit = jnp.where(lane >= part * (width // parts), support_ref[part] * GROUP_CH, limit)
    return limit


def mask_taps(parts, limit):
    lag_pos = lax.broadcasted_iota(jnp.int32, parts[0].shape, 0)
    return [jnp.where(lag_pos < limit, part, 0.0).astype(BF16) for part in parts]


def fast_kernel(lags, piece, support_ref, mixed_ref, table_ref, fwd_hi, fwd_lo, inv_hi, inv_lo, out_ref):
    devices, rows, width = mixed_ref.shape
    seq_count = devices // 4
    own = (rows - 2 * piece) // 2
    per_block = lags // (4 * piece)
    limit = lane_limit(support_ref, width)
    table = table_ref[...]

    def gathered(at):
        moved = swap_blocks(
            [[mixed_ref[s * 4 + c, at : at + piece, :] for c in range(4)] for s in range(seq_count)], table
        )
        flat = [part for parts in moved for part in parts]
        size = 4 * per_block
        return [jnp.concatenate(flat[k : k + size], axis=0) for k in range(0, len(flat), size)]

    tap_parts = mixed_ref[:, 2 * piece :, :].astype(F32)
    taps = mask_taps([tap_parts[:, i * own : (i + 1) * own].reshape(lags, width) for i in range(2)], limit)
    results, filter_grad = conv_grads(
        lags, gathered(0), gathered(piece), taps, limit, (fwd_hi[...], fwd_lo[...]), (inv_hi[...], inv_lo[...])
    )
    for j in range(devices):
        out_ref[j, piece:, :] = split_rows(filter_grad[j * own : (j + 1) * own])
    stacks = []
    for s in range(seq_count):
        result = results[s // per_block].astype(BF16)
        start = (s % per_block) * 4 * piece
        stacks.append([result[start + q * piece : start + (q + 1) * piece] for q in range(4)])
    moved = swap_blocks(stacks, table)
    for s in range(seq_count):
        for c in range(4):
            out_ref[s * 4 + c, 0:piece, :] = moved[s][c]


def unpack_kernel(mixed_ref, table_ref, out_hbm, filter_hbm, out_ref, filter_ref, sems):
    rows, width_here = out_ref.shape
    piece = rows // 4
    own = filter_ref.shape[0]
    tiles = range(width_here // LANES)
    table = table_ref[...]
    moved = swap_blocks([[mixed_ref[tile * 4 + l, 0:piece, :] for l in range(4)] for tile in tiles], table)
    for tile in tiles:
        for q in range(4):
            out_ref[q * piece : (q + 1) * piece, tile * LANES : (tile + 1) * LANES] = moved[tile][q]
    first = pltpu.make_async_copy(out_ref, out_hbm, sems.at[0])
    first.start()
    moved = swap_blocks([[mixed_ref[tile * 4 + l, piece:, :] for l in range(4)] for tile in tiles], table)
    for tile in tiles:
        for c in range(4):
            both = moved[tile][c].astype(F32)
            start = c * width_here + tile * LANES
            filter_ref[:, start : start + LANES] = both[:own] + both[own:]
    second = pltpu.make_async_copy(filter_ref, filter_hbm, sems.at[1])
    second.start()
    first.wait()
    second.wait()


def fast_body(inputs, grads, filter_taps, supports, seq_count, chan_count):
    block_len, width_here = inputs.shape
    rows_each = filter_taps.shape[0]
    devices = seq_count * chan_count
    lags = rows_each * devices
    piece = block_len // 4
    table = swap_table()
    groups_here = width_here // GROUP_CH
    own_support = lax.dynamic_slice_in_dim(
        supports.reshape(chan_count, groups_here), lax.axis_index("seq"), 1, 1
    ).reshape(chan_count)
    mixed = pl.pallas_call(
        pack_kernel,
        out_shape=jax.ShapeDtypeStruct((devices, 2 * piece + 2 * rows_each, LANES), BF16),
        in_specs=[HBM] * 4, out_specs=VMEM,
        scratch_shapes=[
            pltpu.VMEM(inputs.shape, BF16), pltpu.VMEM(inputs.shape, BF16),
            pltpu.VMEM(filter_taps.shape, F32), pltpu.VMEM(table.shape, BF16),
            pltpu.SemaphoreType.DMA((4,)),
        ],
        compiler_params=PARAMS, name="pack",
    )(grads, inputs, filter_taps, table)
    mixed = lax.all_to_all(mixed, EVERY, split_axis=0, concat_axis=0, tiled=True)
    mixed = pl.pallas_call(
        functools.partial(fast_kernel, lags, piece),
        out_shape=jax.ShapeDtypeStruct((devices, piece + 2 * rows_each, LANES), BF16),
        in_specs=[SMEM] + [VMEM] * 6, out_specs=VMEM, compiler_params=PARAMS, name="conv_grads",
    )(own_support, mixed, table, *tables(lags))
    mixed = lax.all_to_all(mixed, EVERY, split_axis=0, concat_axis=0, tiled=True)
    return pl.pallas_call(
        unpack_kernel,
        out_shape=(
            jax.ShapeDtypeStruct((block_len, width_here), BF16),
            jax.ShapeDtypeStruct(filter_taps.shape, F32),
        ),
        in_specs=[VMEM] * 2, out_specs=(HBM, HBM),
        scratch_shapes=[
            pltpu.VMEM((block_len, width_here), BF16), pltpu.VMEM(filter_taps.shape, F32),
            pltpu.SemaphoreType.DMA((2,)),
        ],
        compiler_params=PARAMS, name="unpack",
    )(mixed, table)


def plain_kernel(
    lags, support_ref, grad_ref, signal_ref, high_ref, low_ref, fwd_hi, fwd_lo, inv_hi, inv_lo, out_ref, filter_ref
):
    total, width = grad_ref.shape
    limit = lane_limit(support_ref, width)
    taps = mask_taps([high_ref[...].astype(F32), low_ref[...].astype(F32)], limit)
    cuts = [slice(k * lags, (k + 1) * lags) for k in range(total // lags)]
    results, filter_grad = conv_grads(
        lags, [grad_ref[cut, :] for cut in cuts], [signal_ref[cut, :] for cut in cuts], taps, limit,
        (fwd_hi[...], fwd_lo[...]), (inv_hi[...], inv_lo[...]),
    )
    for cut, result in zip(cuts, results):
        out_ref[cut, :] = result.astype(BF16)
    filter_ref[...] = filter_grad


def plain_body(inputs, grads, filter_taps, supports, seq_count, chan_count):
    block_len, width_here = inputs.shape
    rows_each = filter_taps.shape[0]
    devices = seq_count * chan_count
    lags = rows_each * devices
    total = block_len * seq_count
    share = width_here // devices
    width = share * chan_count
    index = lax.axis_index("seq") * chan_count + lax.axis_index("chan")
    groups_here = width_here // GROUP_CH
    own_support = lax.dynamic_slice_in_dim(
        supports.reshape(chan_count, groups_here), index * share // GROUP_CH, 1, 1
    ).reshape(chan_count)

    def sent(values):
        return values.reshape(block_len, devices, share).transpose(1, 0, 2).reshape(devices, -1)

    def received(values):
        return values.reshape(seq_count, chan_count, block_len, share).transpose(0, 2, 1, 3).reshape(total, width)

    taps = filter_taps.reshape(rows_each, chan_count, devices, share).transpose(2, 0, 1, 3).reshape(devices, -1)
    mixed = jnp.concatenate([sent(grads), sent(inputs), *split_outside(taps)], axis=1)
    mixed = lax.all_to_all(mixed, EVERY, split_axis=0, concat_axis=0, tiled=True)
    part, own = block_len * share, rows_each * width
    upstream, signal = received(mixed[:, :part]), received(mixed[:, part : 2 * part])
    taps_high = mixed[:, 2 * part : 2 * part + own].reshape(lags, width)
    taps_low = mixed[:, 2 * part + own :].reshape(lags, width)
    result, filter_grad = pl.pallas_call(
        functools.partial(plain_kernel, lags),
        out_shape=(jax.ShapeDtypeStruct((total, width), BF16), jax.ShapeDtypeStruct((lags, width), F32)),
        in_specs=[SMEM] + [VMEM] * 8, out_specs=(VMEM, VMEM), compiler_params=PARAMS, name="conv_grads",
    )(own_support, upstream, signal, taps_high, taps_low, *tables(lags))
    result = result.reshape(seq_count, block_len, chan_count, share).transpose(0, 2, 1, 3).reshape(devices, part)
    mixed = jnp.concatenate([result, *split_outside(filter_grad.reshape(devices, own))], axis=1)
    mixed = lax.all_to_all(mixed, EVERY, split_axis=0, concat_axis=0, tiled=True)
    grad_inputs = mixed[:, :part].reshape(devices, block_len, share).transpose(1, 0, 2).reshape(block_len, width_here)
    filter_grad = mixed[:, part : part + own].astype(F32) + mixed[:, part + own :].astype(F32)
    filter_grad = filter_grad.reshape(devices, rows_each, chan_count, share).transpose(1, 2, 0, 3)
    return grad_inputs, filter_grad.reshape(filter_taps.shape)


def solution(mesh):
    seq_count, chan_count = mesh.shape["seq"], mesh.shape["chan"]

    def body(inputs, grads, filter_taps, supports):
        share = inputs.shape[1] // (seq_count * chan_count)
        lags = filter_taps.shape[0] * seq_count * chan_count
        fits = chan_count == 4 and share * 4 == LANES and filter_taps.shape[0] % 8 == 0
        fits = fits and inputs.shape[0] % 64 == 0 and lags % inputs.shape[0] == 0
        chosen = fast_body if fits else plain_body
        return chosen(inputs, grads, filter_taps, supports, seq_count, chan_count)

    in_specs = (P("seq", "chan"), P("seq", "chan"), P(("seq", "chan"), None), P())
    out_specs = (P("seq", "chan"), P(("seq", "chan"), None))
    return jax.shard_map(body, mesh=mesh, in_specs=in_specs, out_specs=out_specs, check_vma=False)
```

time: 207 us -> 52.9 us (0.26)
  waiting for transfers between devices: 119 us -> 17 us
  matrix products: 21.7 us -> 0 us
  other arithmetic: 19.8 us -> 0 us
  between operations: 14.2 us -> 0.73 us
  blocking collectives: 9.4 us -> 16.5 us
  Pallas kernels: 0 us -> 6.26 us
  starting transfers between devices: 12.7 us -> 7.29 us
  local copies, waits for them, and re-layouts: 9.5 us -> 4.79 us
    reduce_scatter x1 -> x0, waiting for transfers between devices: 63.8 us -> none  [body(): lax.psum_scatter(filter_term, 'seq', scatter_dimension=0, tiled=True)]
    all_gather x1 -> x0, waiting for transfers between devices: 35.1 us -> none  [body(): all_taps = lax.all_gather(own_taps, 'seq', axis=0, tiled=True)]
    dot_general x13 -> x0, matrix products: 21.7 us -> none  [apply_table(): jnp.dot(table, values, precision=HIGHEST, preferred_element_type=jnp.floa...]
    ppermute x4 -> x0, waiting for transfers between devices: 17.2 us -> none  [passed_along(): return lax.ppermute(value, axis, pairs)]
    all_to_all x1, waiting for transfers between devices: 2.6 us -> 17 us  [fast_body(): lax.all_to_all(mixed, EVERY, split_axis=0, concat_axis=0, tiled=True)]
    ppermute x4 -> x0, starting transfers between devices: 9.33 us -> none  [passed_along(): return lax.ppermute(value, axis, pairs)]
    add x7 -> x0, other arithmetic: 7.22 us -> none  [the longest x5 5.87 us: times_conj(): real_part = first_re * second_re + first_im * second_im]
    all_to_all x1, blocking collectives: 9.4 us -> 16.5 us  [fast_body(): lax.all_to_all(mixed, EVERY, split_axis=0, concat_axis=0, tiled=True)]
  transfers between devices with their start and end apart: 7 -> 1, of which waited for: 5 -> 1; matrix products, arithmetic and copies ran while one was open for 7% -> 1% of each run, Pallas kernels for 0% -> 0%
where the time goes in v1:
time: 52.9 us; the launch traced here: 52.6 us
  waiting for transfers between devices  17 us (32%)
  blocking collectives  16.5 us (31%)
  starting transfers between devices  7.29 us (14%)
  Pallas kernels  6.26 us (12%)
  local copies, waits for them, and re-layouts  4.79 us (9%)
  between operations  0.73 us (1%)
    all_to_all x1, waiting for transfers between devices, fast_body(): lax.all_to_all(mixed, EVERY, split_axis=0, concat_axis=0, tiled=True)  17 us
    all_to_all x1, blocking collectives, fast_body(): lax.all_to_all(mixed, EVERY, split_axis=0, concat_axis=0, tiled=True)  16.5 us
    all_to_all x1, starting transfers between devices, fast_body(): lax.all_to_all(mixed, EVERY, split_axis=0, concat_axis=0, tiled=True)  7.29 us
    unnamed x20, local copies, waits for them, and re-layouts  4.52 us
    pallas_call x1, Pallas kernels, fast_body(): pl.pallas_call(functools.partial(fast_kernel, lags, piece), out_shape=jax...  3.19 us
    pallas_call x1, Pallas kernels, fast_body(): pl.pallas_call(pack_kernel, out_shape=jax.ShapeDtypeStruct((devices, 2 *...  2 us
    pallas_call x1, Pallas kernels, fast_body(): pl.pallas_call(unpack_kernel, out_shape=(jax.ShapeDtypeStruct((block_len,...  1.07 us
  transfers between devices with their start and end apart: 1, of which 1 were waited for; matrix products, arithmetic and copies ran while one was open for 1% of the time, Pallas kernels for 0%

profile of v1, /device:TPU:0, one launch (start us, length us, event | category | flops | bytes accessed | tf_op | source)
XLA Modules:
  0.0 52.6 jit_solution(7688922203338557893)
XLA Ops:
  0.6 0.0 copy-start
  0.6 1.0 %copy-done = bf16[512,512]{1,0:T(8,128)(2,1)S(1)} copy-done((bf16[512,512]{1,0:T(8,128)(2,1)S(1)}, bf16[512,512]{1,0:T(8,128)(2,1)}, u32[]{:S(2)}) %copy-start) | copy-done | bytes 524312
  1.7 0.9 %copy-done.2 = bf16[128,1024]{1,0:T(8,128)(2,1)S(1)} copy-done((bf16[128,1024]{1,0:T(8,128)(2,1)S(1)}, bf16[128,1024]{1,0:T(8,128)(2,1)}, u32[]{:S(2)}) %copy-start.2) | copy-done | bytes 262168
  2.6 0.9 %copy-done.3 = bf16[128,1024]{1,0:T(8,128)(2,1)S(1)} copy-done((bf16[128,1024]{1,0:T(8,128)(2,1)S(1)}, bf16[128,1024]{1,0:T(8,128)(2,1)}, u32[]{:S(2)}) %copy-start.3) | copy-done | bytes 262168
  3.6 0.9 %copy-done.8 = f32[8,4096]{1,0:T(8,128)S(1)} copy-done((f32[8,4096]{1,0:T(8,128)S(1)}, f32[8,4096]{1,0:T(8,128)}, u32[]{:S(2)}) %copy-start.8) | copy-done | bytes 131096
  4.5 2.0 %pack.1 = bf16[32,80,128]{2,1,0:T(8,128)(2,1)} custom-call(bf16[128,1024]{1,0:T(8,128)(2,1)S(1)} %copy-done.2, bf16[128,1024]{1,0:T(8,128)(2,1)S(1)} %copy-done.3, f32[8,4096]{1,0:T(8,128)S(1)} %copy-done.8, bf16[512,512]{1,0:T(8,128)(2,1)S(1)} %copy-done), custom_call_target="tpu_custom_call" | custom-call | tf_op jit(solution)/shard_map/pack/pallas_call | solution.py:238
  6.5 0.0 copy-start.1
  6.5 0.0 copy-start.4
  6.5 0.0 copy-start.5
  6.5 0.0 copy-start.6
  6.5 7.3 %all-to-all-start = ((bf16[32,80,128]{2,1,0:T(8,128)(2,1)}), bf16[32,80,128]{2,1,0:T(8,128)(2,1)S(1)}, u32[]{:S(2)}, u32[]{:S(2)}) async-start(bf16[32,80,128]{2,1,0:T(8,128)(2,1)} %pack.1), calls=%async_computation | async-start | bytes 1310720 | tf_op jit(solution)/shard_map/all_to_all | solution.py:249
  13.8 0.0 copy-start.9
  13.9 0.6 %copy-done.9 = s32[32]{0:T(128)S(1)} copy-done((s32[32]{0:T(128)S(1)}, s32[32]{0:T(128)}, u32[]{:S(2)}) %copy-start.9) | copy-done | bytes 152
  14.5 0.1 reshape.10
  14.6 0.2 dynamic-slice_reduce_fusion.support_ref
  14.8 17.0 %all-to-all-done.mixed_ref = bf16[32,80,128]{2,1,0:T(8,128)(2,1)S(1)} async-done(((bf16[32,80,128]{2,1,0:T(8,128)(2,1)}), bf16[32,80,128]{2,1,0:T(8,128)(2,1)S(1)}, u32[]{:S(2)}, u32[]{:S(2)}) %all-to-all-start) | async-done | bytes 655392 | tf_op jit(solution)/shard_map/all_to_all | solution.py:249
  31.8 0.0 copy-done.7
  31.8 0.0 copy-done.1
  31.8 0.0 copy-done.4
  31.8 0.0 copy-done.5
  31.8 0.0 copy-done.6
  31.8 3.2 %conv_grads.1 = bf16[32,48,128]{2,1,0:T(8,128)(2,1)S(1)} custom-call(s32[4]{0:T(128)S(1)} %dynamic-slice_reduce_fusion.support_ref, bf16[32,80,128]{2,1,0:T(8,128)(2,1)S(1)} %all-to-all-done.mixed_ref, bf16[512,512]{1,0:T(8,128)(2,1)S(1)} %copy-done.1, bf16[512,256]{1,0:T(8,128)(2,1)S(1)} %copy-done.7, bf16[512,256]{1,0:T(8,128)(2,1)S(1)} %copy-done.6, ...), custom_call_target="tpu_custom_call" | custom-call | tf_op jit(solution)/shard_map/conv_grads/pallas_call | solution.py:250
  35.0 16.5 %all_to_all.10.mixed_ref = bf16[32,48,128]{2,1,0:T(8,128)(2,1)S(1)} all-to-all(bf16[32,48,128]{2,1,0:T(8,128)(2,1)S(1)} %conv_grads.1), channel_id=1, replica_groups=mesh['seq'=8,'chan'=4] {'seq','chan'}, dimensions={0} | all-to-all | bytes 786432 | tf_op jit(solution)/shard_map/all_to_all | solution.py:255
  51.5 1.1 %unpack.1 = (bf16[128,1024]{1,0:T(8,128)(2,1)}, f32[8,4096]{1,0:T(8,128)}) custom-call(bf16[32,48,128]{2,1,0:T(8,128)(2,1)S(1)} %all_to_all.10.mixed_ref, bf16[512,512]{1,0:T(8,128)(2,1)S(1)} %copy-done.1), custom_call_target="tpu_custom_call" | custom-call | tf_op jit(solution)/shard_map/unpack/pallas_call | solution.py:256
  (4 shorter events, 0.0 us)
Async XLA Ops:
  0.6 1.0 %copy-start = (bf16[512,512]{1,0:T(8,128)(2,1)S(1)}, bf16[512,512]{1,0:T(8,128)(2,1)}, u32[]{:S(2)}) copy-start(bf16[512,512]{1,0:T(8,128)(2,1)} %constant.20.clone.table_hbm.table_ref) | copy-start | bytes 1572868
  1.7 0.9 %copy-start.2 = (bf16[128,1024]{1,0:T(8,128)(2,1)S(1)}, bf16[128,1024]{1,0:T(8,128)(2,1)}, u32[]{:S(2)}) copy-start(bf16[128,1024]{1,0:T(8,128)(2,1)} %grad_hbm.1) | copy-start | bytes 786436
  2.6 0.9 %copy-start.3 = (bf16[128,1024]{1,0:T(8,128)(2,1)S(1)}, bf16[128,1024]{1,0:T(8,128)(2,1)}, u32[]{:S(2)}) copy-start(bf16[128,1024]{1,0:T(8,128)(2,1)} %signal_hbm.1) | copy-start | bytes 786436
  3.6 0.9 %copy-start.8 = (f32[8,4096]{1,0:T(8,128)S(1)}, f32[8,4096]{1,0:T(8,128)}, u32[]{:S(2)}) copy-start(f32[8,4096]{1,0:T(8,128)} %taps_hbm.1) | copy-start | bytes 393220
  4.5 27.3 %copy-start.7 = (bf16[512,256]{1,0:T(8,128)(2,1)S(1)}, bf16[512,256]{1,0:T(8,128)(2,1)}, u32[]{:S(2)}) copy-start(bf16[512,256]{1,0:T(8,128)(2,1)} %constant.21.clone.fwd_hi) | copy-start | bytes 786436
  6.5 25.3 %copy-start.1 = (bf16[512,512]{1,0:T(8,128)(2,1)S(1)}, bf16[512,512]{1,0:T(8,128)(2,1)}, u32[]{:S(2)}) copy-start(bf16[512,512]{1,0:T(8,128)(2,1)} %constant.20.clone.table_hbm.table_ref) | copy-start | bytes 1572868
  6.5 25.3 %copy-start.4 = (bf16[256,512]{1,0:T(8,128)(2,1)S(1)}, bf16[256,512]{1,0:T(8,128)(2,1)}, u32[]{:S(2)}) copy-start(bf16[256,512]{1,0:T(8,128)(2,1)} %constant.24.clone.inv_lo) | copy-start | bytes 786436
  6.5 25.3 %copy-start.5 = (bf16[256,512]{1,0:T(8,128)(2,1)S(1)}, bf16[256,512]{1,0:T(8,128)(2,1)}, u32[]{:S(2)}) copy-start(bf16[256,512]{1,0:T(8,128)(2,1)} %constant.23.clone.inv_hi) | copy-start | bytes 786436
  6.5 25.2 %copy-start.6 = (bf16[512,256]{1,0:T(8,128)(2,1)S(1)}, bf16[512,256]{1,0:T(8,128)(2,1)}, u32[]{:S(2)}) copy-start(bf16[512,256]{1,0:T(8,128)(2,1)} %constant.22.clone.fwd_lo) | copy-start | bytes 786436
  6.5 25.2 %all-to-all-start = ((bf16[32,80,128]{2,1,0:T(8,128)(2,1)}), bf16[32,80,128]{2,1,0:T(8,128)(2,1)S(1)}, u32[]{:S(2)}, u32[]{:S(2)}) async-start(bf16[32,80,128]{2,1,0:T(8,128)(2,1)} %pack.1), calls=%async_computation | async-start | bytes 1310720 | tf_op jit(solution)/shard_map/all_to_all | solution.py:249
  13.8 0.7 %copy-start.9 = (s32[32]{0:T(128)S(1)}, s32[32]{0:T(128)}, u32[]{:S(2)}) copy-start(s32[32]{0:T(128)} %param.12) | copy-start | bytes 388

commit v2 on v1

--- a/solution.py
+++ b/solution.py
@@ -30,8 +30,10 @@
     freqs = np.concatenate([np.arange(0, lags, 2), np.arange(1, lags, 2)]) + 0.5
     angle = freqs[:, None] * np.arange(lags)[None, :] * (np.pi / lags)
     forward = np.concatenate([np.cos(angle), -np.sin(angle)], axis=0)
-    parts = split_table(forward) + split_table(forward.T / lags)
-    return [jnp.asarray(part) for part in parts]
+    high, low = split_table(forward)
+    back_high, back_low = split_table(forward.T / lags)
+    joined = (np.concatenate([high, low], axis=1), np.concatenate([back_high, back_high, back_low], axis=1))
+    return [jnp.asarray(part) for part in joined]
 
 
 def split_values(values):
@@ -49,12 +51,12 @@
 
 
 def dot_exact(table, values):
-    return dot(table[0], values) + dot(table[1], values)
+    return dot(table, jnp.concatenate([values, values], axis=0))
 
 
 def dot_split(table, values):
     high, low = split_values(values)
-    return dot(table[0], high) + (dot(table[0], low) + dot(table[1], high))
+    return dot(table, jnp.concatenate([high, low, high], axis=0))
 
 
 def conj_product(first, second, half):
@@ -122,34 +124,45 @@
     return jnp.concatenate([high, values - high], axis=0).astype(BF16)
 
 
-def pack_kernel(grad_hbm, signal_hbm, taps_hbm, table_hbm, out_ref, grad_ref, signal_ref, taps_ref, table_ref, sems):
+def pack_kernel(
+    grad_hbm, signal_hbm, taps_hbm, table_hbm, out_hbm, grad_ref, signal_ref, taps_ref, table_ref, out_ref, sems
+):
     pairs = ((table_hbm, table_ref), (grad_hbm, grad_ref), (signal_hbm, signal_ref), (taps_hbm, taps_ref))
-    copies = [pltpu.make_async_copy(source, target, sems.at[i]) for i, (source, target) in enumerate(pairs)]
-    for copy in copies:
+    arriving = [pltpu.make_async_copy(source, target, sems.at[i]) for i, (source, target) in enumerate(pairs)]
+    for copy in arriving:
         copy.start()
     rows, width_here = grad_ref.shape
     piece = rows // 4
     tiles = range(width_here // LANES)
-    copies[0].wait()
+    cuts = [slice(0, piece), slice(piece, 2 * piece), slice(2 * piece, out_ref.shape[1])]
+    leaving = [
+        pltpu.make_async_copy(out_ref.at[:, cut, :], out_hbm.at[:, cut, :], sems.at[4 + i])
+        for i, cut in enumerate(cuts)
+    ]
+
+    def moved_out(index, stacks):
+        moved = swap_blocks(stacks, table)
+        for tile in tiles:
+            for l in range(4):
+                out_ref[tile * 4 + l, cuts[index], :] = moved[tile][l]
+        leaving[index].start()
+
+    arriving[0].wait()
     table = table_ref[...]
-    for at, source, copy in ((0, grad_ref, copies[1]), (piece, signal_ref, copies[2])):
-        copy.wait()
-        moved = swap_blocks(
+    for index, source in enumerate((grad_ref, signal_ref)):
+        arriving[1 + index].wait()
+        moved_out(
+            index,
             [
                 [source[q * piece : (q + 1) * piece, tile * LANES : (tile + 1) * LANES] for q in range(4)]
                 for tile in tiles
             ],
-            table,
         )
-        for tile in tiles:
-            for l in range(4):
-                out_ref[tile * 4 + l, at : at + piece, :] = moved[tile][l]
-    copies[3].wait()
+    arriving[3].wait()
     starts = [[c * width_here + tile * LANES for c in range(4)] for tile in tiles]
-    moved = swap_blocks([[split_rows(taps_ref[:, at : at + LANES]) for at in row] for row in starts], table)
-    for tile in tiles:
-        for l in range(4):
-            out_ref[tile * 4 + l, 2 * piece :, :] = moved[tile][l]
+    moved_out(2, [[split_rows(taps_ref[:, at : at + LANES]) for at in row] for row in starts])
+    for copy in leaving:
+        copy.wait()
 
 
 def lane_limit(support_ref, width):
@@ -166,7 +179,7 @@
     return [jnp.where(lag_pos < limit, part, 0.0).astype(BF16) for part in parts]
 
 
-def fast_kernel(lags, piece, support_ref, mixed_ref, table_ref, fwd_hi, fwd_lo, inv_hi, inv_lo, out_ref):
+def fast_kernel(lags, piece, support_ref, mixed_ref, table_ref, forward_ref, inverse_ref, out_ref):
     devices, rows, width = mixed_ref.shape
     seq_count = devices // 4
     own = (rows - 2 * piece) // 2
@@ -185,7 +198,7 @@
     tap_parts = mixed_ref[:, 2 * piece :, :].astype(F32)
     taps = mask_taps([tap_parts[:, i * own : (i + 1) * own].reshape(lags, width) for i in range(2)], limit)
     results, filter_grad = conv_grads(
-        lags, gathered(0), gathered(piece), taps, limit, (fwd_hi[...], fwd_lo[...]), (inv_hi[...], inv_lo[...])
+        lags, gathered(0), gathered(piece), taps, limit, forward_ref[...], inverse_ref[...]
     )
     for j in range(devices):
         out_ref[j, piece:, :] = split_rows(filter_grad[j * own : (j + 1) * own])
@@ -238,19 +251,20 @@
     mixed = pl.pallas_call(
         pack_kernel,
         out_shape=jax.ShapeDtypeStruct((devices, 2 * piece + 2 * rows_each, LANES), BF16),
-        in_specs=[HBM] * 4, out_specs=VMEM,
+        in_specs=[HBM] * 4, out_specs=HBM,
         scratch_shapes=[
             pltpu.VMEM(inputs.shape, BF16), pltpu.VMEM(inputs.shape, BF16),
             pltpu.VMEM(filter_taps.shape, F32), pltpu.VMEM(table.shape, BF16),
-            pltpu.SemaphoreType.DMA((4,)),
+            pltpu.VMEM((devices, 2 * piece + 2 * rows_each, LANES), BF16),
+            pltpu.SemaphoreType.DMA((7,)),
         ],
-        compiler_params=PARAMS, name="pack",
+        compiler_params=pltpu.CompilerParams(vmem_limit_bytes=60 * 1024 * 1024), name="pack",
     )(grads, inputs, filter_taps, table)
     mixed = lax.all_to_all(mixed, EVERY, split_axis=0, concat_axis=0, tiled=True)
     mixed = pl.pallas_call(
         functools.partial(fast_kernel, lags, piece),
         out_shape=jax.ShapeDtypeStruct((devices, piece + 2 * rows_each, LANES), BF16),
-        in_specs=[SMEM] + [VMEM] * 6, out_specs=VMEM, compiler_params=PARAMS, name="conv_grads",
+        in_specs=[SMEM] + [VMEM] * 4, out_specs=VMEM, compiler_params=PARAMS, name="conv_grads",
     )(own_support, mixed, table, *tables(lags))
     mixed = lax.all_to_all(mixed, EVERY, split_axis=0, concat_axis=0, tiled=True)
     return pl.pallas_call(
@@ -269,7 +283,7 @@
 
 
 def plain_kernel(
-    lags, support_ref, grad_ref, signal_ref, high_ref, low_ref, fwd_hi, fwd_lo, inv_hi, inv_lo, out_ref, filter_ref
+    lags, support_ref, grad_ref, signal_ref, high_ref, low_ref, forward_ref, inverse_ref, out_ref, filter_ref
 ):
     total, width = grad_ref.shape
     limit = lane_limit(support_ref, width)
@@ -277,7 +291,7 @@
     cuts = [slice(k * lags, (k + 1) * lags) for k in range(total // lags)]
     results, filter_grad = conv_grads(
         lags, [grad_ref[cut, :] for cut in cuts], [signal_ref[cut, :] for cut in cuts], taps, limit,
-        (fwd_hi[...], fwd_lo[...]), (inv_hi[...], inv_lo[...]),
+        forward_ref[...], inverse_ref[...],
     )
     for cut, result in zip(cuts, results):
         out_ref[cut, :] = result.astype(BF16)
@@ -314,7 +328,7 @@
     result, filter_grad = pl.pallas_call(
         functools.partial(plain_kernel, lags),
         out_shape=(jax.ShapeDtypeStruct((total, width), BF16), jax.ShapeDtypeStruct((lags, width), F32)),
-        in_specs=[SMEM] + [VMEM] * 8, out_specs=(VMEM, VMEM), compiler_params=PARAMS, name="conv_grads",
+        in_specs=[SMEM] + [VMEM] * 6, out_specs=(VMEM, VMEM), compiler_params=PARAMS, name="conv_grads",
     )(own_support, upstream, signal, taps_high, taps_low, *tables(lags))
     result = result.reshape(seq_count, block_len, chan_count, share).transpose(0, 2, 1, 3).reshape(devices, part)
     mixed = jnp.concatenate([result, *split_outside(filter_grad.reshape(devices, own))], axis=1)

time: 52.9 us -> 49.4 us (0.934)
  local copies, waits for them, and re-layouts: 4.79 us -> 0.94 us
    unnamed x20 -> x8, local copies, waits for them, and re-layouts: 4.52 us -> 0.67 us
    pallas_call x1, Pallas kernels: 2 us -> 2.74 us  [fast_body(): pl.pallas_call(pack_kernel, out_shape=jax.ShapeDtypeStruct((devices, 2 *...]
where the time goes in v2:
time: 49.4 us; the launch traced here: 49.2 us
  waiting for transfers between devices  17 us (34%)
  blocking collectives  16.5 us (33%)
  starting transfers between devices  7.3 us (15%)
  Pallas kernels  6.74 us (14%)
  local copies, waits for them, and re-layouts  0.94 us (2%)
  between operations  0.7 us (1%)
    all_to_all x1, waiting for transfers between devices, fast_body(): lax.all_to_all(mixed, EVERY, split_axis=0, concat_axis=0, tiled=True)  17 us
    all_to_all x1, blocking collectives, fast_body(): lax.all_to_all(mixed, EVERY, split_axis=0, concat_axis=0, tiled=True)  16.5 us
    all_to_all x1, starting transfers between devices, fast_body(): lax.all_to_all(mixed, EVERY, split_axis=0, concat_axis=0, tiled=True)  7.3 us
    pallas_call x1, Pallas kernels, fast_body(): pl.pallas_call(functools.partial(fast_kernel, lags, piece), out_shape=jax...  2.93 us
    pallas_call x1, Pallas kernels, fast_body(): pl.pallas_call(pack_kernel, out_shape=jax.ShapeDtypeStruct((devices, 2 *...  2.74 us
    pallas_call x1, Pallas kernels, fast_body(): pl.pallas_call(unpack_kernel, out_shape=(jax.ShapeDtypeStruct((block_len,...  1.07 us
  transfers between devices with their start and end apart: 1, of which 1 were waited for; matrix products, arithmetic and copies ran while one was open for 1% of the time, Pallas kernels for 0%

profile of v2, /device:TPU:0, one launch (start us, length us, event | category | flops | bytes accessed | tf_op | source)
XLA Modules:
  0.0 49.2 jit_solution(17157577344551902778)
XLA Ops:
  0.6 0.0 copy-start.2
  0.6 2.7 %pack.1 = bf16[32,80,128]{2,1,0:T(8,128)(2,1)} custom-call(bf16[128,1024]{1,0:T(8,128)(2,1)} %grad_hbm.1, bf16[128,1024]{1,0:T(8,128)(2,1)} %signal_hbm.1, f32[8,4096]{1,0:T(8,128)} %taps_hbm.1, bf16[512,512]{1,0:T(8,128)(2,1)} %constant.16.clone.table_hbm.table_ref), custom_call_target="tpu_custom_call" | custom-call | tf_op jit(solution)/shard_map/pack/pallas_call | solution.py:251
  3.4 0.0 copy-start
  3.4 0.0 copy-start.1
  3.4 7.3 %all-to-all-start = ((bf16[32,80,128]{2,1,0:T(8,128)(2,1)}), bf16[32,80,128]{2,1,0:T(8,128)(2,1)S(1)}, u32[]{:S(2)}, u32[]{:S(2)}) async-start(bf16[32,80,128]{2,1,0:T(8,128)(2,1)} %pack.1), calls=%async_computation | async-start | bytes 1310720 | tf_op jit(solution)/shard_map/all_to_all | solution.py:263
  10.7 0.0 copy-start.3
  10.7 0.6 %copy-done.3 = s32[32]{0:T(128)S(1)} copy-done((s32[32]{0:T(128)S(1)}, s32[32]{0:T(128)}, u32[]{:S(2)}) %copy-start.3) | copy-done | bytes 152
  11.4 0.1 reshape.10
  11.5 0.2 dynamic-slice_reduce_fusion.support_ref
  11.7 17.0 %all-to-all-done.mixed_ref = bf16[32,80,128]{2,1,0:T(8,128)(2,1)S(1)} async-done(((bf16[32,80,128]{2,1,0:T(8,128)(2,1)}), bf16[32,80,128]{2,1,0:T(8,128)(2,1)S(1)}, u32[]{:S(2)}, u32[]{:S(2)}) %all-to-all-start) | async-done | bytes 655392 | tf_op jit(solution)/shard_map/all_to_all | solution.py:263
  28.6 0.0 copy-done.2
  28.6 0.0 copy-done
  28.6 0.0 copy-done.1
  28.7 2.9 %conv_grads.1 = bf16[32,48,128]{2,1,0:T(8,128)(2,1)S(1)} custom-call(s32[4]{0:T(128)S(1)} %dynamic-slice_reduce_fusion.support_ref, bf16[32,80,128]{2,1,0:T(8,128)(2,1)S(1)} %all-to-all-done.mixed_ref, bf16[512,512]{1,0:T(8,128)(2,1)S(1)} %copy-done, bf16[512,512]{1,0:T(8,128)(2,1)S(1)} %copy-done.2, bf16[256,1536]{1,0:T(8,128)(2,1)S(1)} %copy-done.1), custom_call_target="tpu_custom_call" | custom-call | tf_op jit(solution)/shard_map/conv_grads/pallas_call | solution.py:264
  31.6 16.5 %all_to_all.10.mixed_ref = bf16[32,48,128]{2,1,0:T(8,128)(2,1)S(1)} all-to-all(bf16[32,48,128]{2,1,0:T(8,128)(2,1)S(1)} %conv_grads.1), channel_id=1, replica_groups=mesh['seq'=8,'chan'=4] {'seq','chan'}, dimensions={0} | all-to-all | bytes 786432 | tf_op jit(solution)/shard_map/all_to_all | solution.py:269
  48.1 1.1 %unpack.1 = (bf16[128,1024]{1,0:T(8,128)(2,1)}, f32[8,4096]{1,0:T(8,128)}) custom-call(bf16[32,48,128]{2,1,0:T(8,128)(2,1)S(1)} %all_to_all.10.mixed_ref, bf16[512,512]{1,0:T(8,128)(2,1)S(1)} %copy-done), custom_call_target="tpu_custom_call" | custom-call | tf_op jit(solution)/shard_map/unpack/pallas_call | solution.py:270
Async XLA Ops:
  0.6 28.0 %copy-start.2 = (bf16[512,512]{1,0:T(8,128)(2,1)S(1)}, bf16[512,512]{1,0:T(8,128)(2,1)}, u32[]{:S(2)}) copy-start(bf16[512,512]{1,0:T(8,128)(2,1)} %constant.17.clone.forward_ref) | copy-start | bytes 1572868
  3.4 25.3 %copy-start = (bf16[512,512]{1,0:T(8,128)(2,1)S(1)}, bf16[512,512]{1,0:T(8,128)(2,1)}, u32[]{:S(2)}) copy-start(bf16[512,512]{1,0:T(8,128)(2,1)} %constant.16.clone.table_hbm.table_ref) | copy-start | bytes 1572868
  3.4 25.2 %copy-start.1 = (bf16[256,1536]{1,0:T(8,128)(2,1)S(1)}, bf16[256,1536]{1,0:T(8,128)(2,1)}, u32[]{:S(2)}) copy-start(bf16[256,1536]{1,0:T(8,128)(2,1)} %constant.18.clone.inverse_ref) | copy-start | bytes 2359300
  3.4 25.2 %all-to-all-start = ((bf16[32,80,128]{2,1,0:T(8,128)(2,1)}), bf16[32,80,128]{2,1,0:T(8,128)(2,1)S(1)}, u32[]{:S(2)}, u32[]{:S(2)}) async-start(bf16[32,80,128]{2,1,0:T(8,128)(2,1)} %pack.1), calls=%async_computation | async-start | bytes 1310720 | tf_op jit(solution)/shard_map/all_to_all | solution.py:263
  10.7 0.7 %copy-start.3 = (s32[32]{0:T(128)S(1)}, s32[32]{0:T(128)}, u32[]{:S(2)}) copy-start(s32[32]{0:T(128)} %param.10) | copy-start | bytes 388

commit v3 on v2

--- a/solution.py
+++ b/solution.py
@@ -76,38 +76,48 @@
     )
 
 
+def transform(dot_with, table, parts):
+    width = parts[0].shape[1]
+    group = 2 if width == LANES else 1
+    found = []
+    for i in range(0, len(parts), group):
+        pair = parts[i : i + group]
+        joined = dot_with(table, jnp.concatenate(pair, axis=1) if len(pair) > 1 else pair[0])
+        found += [joined[:, k * width : (k + 1) * width] for k in range(len(pair))]
+    return found
+
+
 def conv_grads(lags, upstream, signal, taps, limit, forward, inverse):
-    blocks, width = len(upstream), upstream[0].shape[1]
-    if width == LANES:
-        joined = dot_exact(forward, jnp.concatenate(upstream + signal + taps, axis=1))
-        specs = [joined[:, k * width : (k + 1) * width] for k in range(2 * blocks + 2)]
-    else:
-        specs = [dot_exact(forward, part) for part in upstream + signal + taps]
-    taps_spec = specs[2 * blocks] + specs[2 * blocks + 1]
-    products, filter_spec = [], None
-    for k in range(blocks):
-        window = add_next(specs[k], specs[k + 1], lags) if k + 1 < blocks else specs[k]
-        products.append(conj_product(window, taps_spec, lags))
-        term = conj_product(window, specs[blocks + k], lags)
-        filter_spec = term if filter_spec is None else filter_spec + term
-    products.append(filter_spec)
-    if width == LANES:
-        joined = dot_split(inverse, jnp.concatenate(products, axis=1))
-        results = [joined[:, k * width : (k + 1) * width] for k in range(blocks + 1)]
-    else:
-        results = [dot_split(inverse, product) for product in products]
-    lag_pos = lax.broadcasted_iota(jnp.int32, results[-1].shape, 0)
-    return results[:-1], jnp.where(lag_pos < limit, results[-1], 0.0)
+    blocks = len(upstream)
+    taps_high, taps_low = transform(dot_exact, forward, taps)
+    taps_spec = taps_high + taps_low
+    specs = transform(dot_exact, forward, upstream)
+    results, filter_spec = [], None
+    for start in range(0, blocks, 2):
+        pair = range(start, min(start + 2, blocks))
+        signal_specs = transform(dot_exact, forward, [signal[k] for k in pair])
+        windows = [add_next(specs[k], specs[k + 1], lags) if k + 1 < blocks else specs[k] for k in pair]
+        results += transform(dot_split, inverse, [conj_product(window, taps_spec, lags) for window in windows])
+        for window, signal_spec in zip(windows, signal_specs):
+            term = conj_product(window, signal_spec, lags)
+            filter_spec = term if filter_spec is None else filter_spec + term
+    (filter_grad,) = transform(dot_split, inverse, [filter_spec])
+    lag_pos = lax.broadcasted_iota(jnp.int32, filter_grad.shape, 0)
+    return results, jnp.where(lag_pos < limit, filter_grad, 0.0)
 
 
 def swap_table():
     quarter = LANES // 4
-    index = np.arange(4 * LANES)
-    part, block, lane = index // LANES, index % LANES // quarter, index % quarter
-    target = block * LANES + part * quarter + lane
-    table = np.zeros((4 * LANES, 4 * LANES), ml_dtypes.bfloat16)
-    table[index, target] = 1
-    return jnp.asarray(table)
+    row = lax.broadcasted_iota(jnp.int32, (quarter, LANES), 0)
+    lane = lax.broadcasted_iota(jnp.int32, (quarter, LANES), 1)
+    zeros = jnp.zeros((quarter, LANES), BF16)
+    slabs = []
+    for part in range(4):
+        pattern = jnp.where(lane == row + part * quarter, 1.0, 0.0).astype(BF16)
+        slabs += [
+            jnp.concatenate([pattern if at == block else zeros for at in range(4)], axis=1) for block in range(4)
+        ]
+    return jnp.concatenate(slabs, axis=0)
 
 
 def swap_blocks(stacks, table):
@@ -124,53 +134,44 @@
     return jnp.concatenate([high, values - high], axis=0).astype(BF16)
 
 
-def pack_kernel(
-    grad_hbm, signal_hbm, taps_hbm, table_hbm, out_hbm, grad_ref, signal_ref, taps_ref, table_ref, out_ref, sems
-):
-    pairs = ((table_hbm, table_ref), (grad_hbm, grad_ref), (signal_hbm, signal_ref), (taps_hbm, taps_ref))
+def pack_kernel(grad_hbm, signal_hbm, taps_hbm, out_ref, grad_ref, signal_ref, taps_ref, sems):
+    pairs = ((grad_hbm, grad_ref), (signal_hbm, signal_ref), (taps_hbm, taps_ref))
     arriving = [pltpu.make_async_copy(source, target, sems.at[i]) for i, (source, target) in enumerate(pairs)]
     for copy in arriving:
         copy.start()
     rows, width_here = grad_ref.shape
     piece = rows // 4
     tiles = range(width_here // LANES)
-    cuts = [slice(0, piece), slice(piece, 2 * piece), slice(2 * piece, out_ref.shape[1])]
-    leaving = [
-        pltpu.make_async_copy(out_ref.at[:, cut, :], out_hbm.at[:, cut, :], sems.at[4 + i])
-        for i, cut in enumerate(cuts)
-    ]
-
-    def moved_out(index, stacks):
+
+    def moved_out(cut, stacks):
         moved = swap_blocks(stacks, table)
         for tile in tiles:
             for l in range(4):
-                out_ref[tile * 4 + l, cuts[index], :] = moved[tile][l]
-        leaving[index].start()
-
-    arriving[0].wait()
-    table = table_ref[...]
+                out_ref[tile * 4 + l, cut, :] = moved[tile][l]
+
+    table = swap_table()
     for index, source in enumerate((grad_ref, signal_ref)):
-        arriving[1 + index].wait()
+        arriving[index].wait()
         moved_out(
-            index,
+            slice(index * piece, (index + 1) * piece),
             [
                 [source[q * piece : (q + 1) * piece, tile * LANES : (tile + 1) * LANES] for q in range(4)]
                 for tile in tiles
             ],
         )
-    arriving[3].wait()
+    arriving[2].wait()
     starts = [[c * width_here + tile * LANES for c in range(4)] for tile in tiles]
-    moved_out(2, [[split_rows(taps_ref[:, at : at + LANES]) for at in row] for row in starts])
-    for copy in leaving:
-        copy.wait()
-
-
-def lane_limit(support_ref, width):
+    moved_out(
+        slice(2 * piece, out_ref.shape[1]),
+        [[split_rows(taps_ref[:, at : at + LANES]) for at in row] for row in starts],
+    )
+
+
+def lane_limit(supports, width):
     lane = lax.broadcasted_iota(jnp.int32, (1, width), 1)
-    parts = support_ref.shape[0]
     limit = jnp.zeros((1, width), jnp.int32)
-    for part in range(parts):
-        limit = jnp.where(lane >= part * (width // parts), support_ref[part] * GROUP_CH, limit)
+    for part, support in enumerate(supports):
+        limit = jnp.where(lane >= part * (width // len(supports)), support * GROUP_CH, limit)
     return limit
 
 
@@ -179,13 +180,16 @@
     return [jnp.where(lag_pos < limit, part, 0.0).astype(BF16) for part in parts]
 
 
-def fast_kernel(lags, piece, support_ref, mixed_ref, table_ref, forward_ref, inverse_ref, out_ref):
+def fast_kernel(
+    lags, piece, support_hbm, mixed_ref, forward_ref, inverse_ref, out_ref, support_ref, sem
+):
+    support_copy = pltpu.make_async_copy(support_hbm, support_ref, sem)
+    support_copy.start()
     devices, rows, width = mixed_ref.shape
     seq_count = devices // 4
     own = (rows - 2 * piece) // 2
     per_block = lags // (4 * piece)
-    limit = lane_limit(support_ref, width)
-    table = table_ref[...]
+    table = swap_table()
 
     def gathered(at):
         moved = swap_blocks(
@@ -195,11 +199,14 @@
         size = 4 * per_block
         return [jnp.concatenate(flat[k : k + size], axis=0) for k in range(0, len(flat), size)]
 
+    upstream, signal = gathered(0), gathered(piece)
     tap_parts = mixed_ref[:, 2 * piece :, :].astype(F32)
+    groups_here = support_ref.shape[0] // 4
+    index = lax.axis_index("seq")
+    support_copy.wait()
+    limit = lane_limit([support_ref[c * groups_here + index] for c in range(4)], width)
     taps = mask_taps([tap_parts[:, i * own : (i + 1) * own].reshape(lags, width) for i in range(2)], limit)
-    results, filter_grad = conv_grads(
-        lags, gathered(0), gathered(piece), taps, limit, forward_ref[...], inverse_ref[...]
-    )
+    results, filter_grad = conv_grads(lags, upstream, signal, taps, limit, forward_ref[...], inverse_ref[...])
     for j in range(devices):
         out_ref[j, piece:, :] = split_rows(filter_grad[j * own : (j + 1) * own])
     stacks = []
@@ -213,12 +220,12 @@
             out_ref[s * 4 + c, 0:piece, :] = moved[s][c]
 
 
-def unpack_kernel(mixed_ref, table_ref, out_hbm, filter_hbm, out_ref, filter_ref, sems):
+def unpack_kernel(mixed_ref, out_hbm, filter_hbm, out_ref, filter_ref, sems):
     rows, width_here = out_ref.shape
     piece = rows // 4
     own = filter_ref.shape[0]
     tiles = range(width_here // LANES)
-    table = table_ref[...]
+    table = swap_table()
     moved = swap_blocks([[mixed_ref[tile * 4 + l, 0:piece, :] for l in range(4)] for tile in tiles], table)
     for tile in tiles:
         for q in range(4):
@@ -243,29 +250,25 @@
     devices = seq_count * chan_count
     lags = rows_each * devices
     piece = block_len // 4
-    table = swap_table()
-    groups_here = width_here // GROUP_CH
-    own_support = lax.dynamic_slice_in_dim(
-        supports.reshape(chan_count, groups_here), lax.axis_index("seq"), 1, 1
-    ).reshape(chan_count)
+    sources = [pltpu.with_memory_space_constraint(part, pltpu.HBM) for part in (grads, inputs, filter_taps)]
     mixed = pl.pallas_call(
         pack_kernel,
-        out_shape=jax.ShapeDtypeStruct((devices, 2 * piece + 2 * rows_each, LANES), BF16),
-        in_specs=[HBM] * 4, out_specs=HBM,
+        out_shape=pltpu.VMEM((devices, 2 * piece + 2 * rows_each, LANES), BF16),
+        in_specs=[HBM] * 3, out_specs=VMEM,
         scratch_shapes=[
             pltpu.VMEM(inputs.shape, BF16), pltpu.VMEM(inputs.shape, BF16),
-            pltpu.VMEM(filter_taps.shape, F32), pltpu.VMEM(table.shape, BF16),
-            pltpu.VMEM((devices, 2 * piece + 2 * rows_each, LANES), BF16),
-            pltpu.SemaphoreType.DMA((7,)),
+            pltpu.VMEM(filter_taps.shape, F32), pltpu.SemaphoreType.DMA((3,)),
         ],
-        compiler_params=pltpu.CompilerParams(vmem_limit_bytes=60 * 1024 * 1024), name="pack",
-    )(grads, inputs, filter_taps, table)
+        compiler_params=PARAMS, name="pack",
+    )(*sources)
     mixed = lax.all_to_all(mixed, EVERY, split_axis=0, concat_axis=0, tiled=True)
     mixed = pl.pallas_call(
         functools.partial(fast_kernel, lags, piece),
         out_shape=jax.ShapeDtypeStruct((devices, piece + 2 * rows_each, LANES), BF16),
-        in_specs=[SMEM] + [VMEM] * 4, out_specs=VMEM, compiler_params=PARAMS, name="conv_grads",
-    )(own_support, mixed, table, *tables(lags))
+        in_specs=[HBM] + [VMEM] * 3, out_specs=VMEM,
+        scratch_shapes=[pltpu.SMEM(supports.shape, jnp.int32), pltpu.SemaphoreType.DMA],
+        compiler_params=PARAMS, name="conv_grads",
+    )(pltpu.with_memory_space_constraint(supports, pltpu.HBM), mixed, *tables(lags))
     mixed = lax.all_to_all(mixed, EVERY, split_axis=0, concat_axis=0, tiled=True)
     return pl.pallas_call(
         unpack_kernel,
@@ -273,20 +276,20 @@
             jax.ShapeDtypeStruct((block_len, width_here), BF16),
             jax.ShapeDtypeStruct(filter_taps.shape, F32),
         ),
-        in_specs=[VMEM] * 2, out_specs=(HBM, HBM),
+        in_specs=[VMEM], out_specs=(HBM, HBM),
         scratch_shapes=[
             pltpu.VMEM((block_len, width_here), BF16), pltpu.VMEM(filter_taps.shape, F32),
             pltpu.SemaphoreType.DMA((2,)),
         ],
         compiler_params=PARAMS, name="unpack",
-    )(mixed, table)
+    )(mixed)
 
 
 def plain_kernel(
     lags, support_ref, grad_ref, signal_ref, high_ref, low_ref, forward_ref, inverse_ref, out_ref, filter_ref
 ):
     total, width = grad_ref.shape
-    limit = lane_limit(support_ref, width)
+    limit = lane_limit([support_ref[part] for part in range(support_ref.shape[0])], width)
     taps = mask_taps([high_ref[...].astype(F32), low_ref[...].astype(F32)], limit)
     cuts = [slice(k * lags, (k + 1) * lags) for k in range(total // lags)]
     results, filter_grad = conv_grads(

time: 49.4 us -> 47.8 us (0.968)
  blocking collectives: 16.5 us -> 41.5 us
  waiting for transfers between devices: 17 us -> 0 us
  starting transfers between devices: 7.3 us -> 0 us
  Pallas kernels: 6.74 us -> 5.37 us
  local copies, waits for them, and re-layouts: 0.94 us -> 0.01 us
    all_to_all x1 -> x2, blocking collectives: 16.5 us -> 41.5 us  [fast_body(): lax.all_to_all(mixed, EVERY, split_axis=0, concat_axis=0, tiled=True)]
    all_to_all x1 -> x0, waiting for transfers between devices: 17 us -> none  [fast_body(): lax.all_to_all(mixed, EVERY, split_axis=0, concat_axis=0, tiled=True)]
    all_to_all x1 -> x0, starting transfers between devices: 7.3 us -> none  [fast_body(): lax.all_to_all(mixed, EVERY, split_axis=0, concat_axis=0, tiled=True)]
    pallas_call x1, Pallas kernels: 2.74 us -> 1.81 us  [fast_body(): pl.pallas_call(pack_kernel, out_shape=pltpu.VMEM((devices, 2 * piece + 2...]
    unnamed x8 -> x4, local copies, waits for them, and re-layouts: 0.67 us -> 0.01 us
  transfers between devices with their start and end apart: 1 -> 0, of which waited for: 1 -> 0; matrix products, arithmetic and copies ran while one was open for 1% -> 0% of each run, Pallas kernels for 0% -> 0%
where the time goes in v3:
time: 47.8 us; the launch traced here: 47.6 us
  blocking collectives  41.5 us (87%)
  Pallas kernels  5.37 us (11%)
  between operations  0.66 us (1%)
    all_to_all x2, blocking collectives, fast_body(): lax.all_to_all(mixed, EVERY, split_axis=0, concat_axis=0, tiled=True)  41.5 us
    pallas_call x1, Pallas kernels, fast_body(): pl.pallas_call(functools.partial(fast_kernel, lags, piece), out_shape=jax...  2.49 us
    pallas_call x1, Pallas kernels, fast_body(): pl.pallas_call(pack_kernel, out_shape=pltpu.VMEM((devices, 2 * piece + 2...  1.81 us
    pallas_call x1, Pallas kernels, fast_body(): pl.pallas_call(unpack_kernel, out_shape=(jax.ShapeDtypeStruct((block_len,...  1.06 us

profile of v3, /device:TPU:0, one launch (start us, length us, event | category | flops | bytes accessed | tf_op | source)
XLA Modules:
  0.0 47.6 jit_solution(8313189004134151349)
XLA Ops:
  0.6 1.8 %pack.1 = bf16[32,80,128]{2,1,0:T(8,128)(2,1)S(1)} custom-call(bf16[128,1024]{1,0:T(8,128)(2,1)} %grad_hbm.1, bf16[128,1024]{1,0:T(8,128)(2,1)} %signal_hbm.1, f32[8,4096]{1,0:T(8,128)} %taps_hbm.1), custom_call_target="tpu_custom_call" | custom-call | tf_op jit(solution)/shard_map/pack/pallas_call | solution.py:254
  2.5 0.0 copy-start
  2.5 0.0 copy-start.1
  2.5 25.0 %all_to_all.10.mixed_ref = bf16[32,80,128]{2,1,0:T(8,128)(2,1)S(1)} all-to-all(bf16[32,80,128]{2,1,0:T(8,128)(2,1)S(1)} %pack.1), channel_id=1, replica_groups=mesh['seq'=8,'chan'=4] {'seq','chan'}, dimensions={0} | all-to-all | bytes 1310720 | tf_op jit(solution)/shard_map/all_to_all | solution.py:264
  27.5 0.0 copy-done
  27.5 0.0 copy-done.1
  27.5 2.5 %conv_grads.1 = bf16[32,48,128]{2,1,0:T(8,128)(2,1)S(1)} custom-call(s32[32]{0:T(128)} %support_hbm.1, bf16[32,80,128]{2,1,0:T(8,128)(2,1)S(1)} %all_to_all.10.mixed_ref, bf16[512,512]{1,0:T(8,128)(2,1)S(1)} %copy-done.1, bf16[256,1536]{1,0:T(8,128)(2,1)S(1)} %copy-done), custom_call_target="tpu_custom_call" | custom-call | tf_op jit(solution)/shard_map/conv_grads/pallas_call | solution.py:265
  30.0 16.5 %all_to_all.11.mixed_ref = bf16[32,48,128]{2,1,0:T(8,128)(2,1)S(1)} all-to-all(bf16[32,48,128]{2,1,0:T(8,128)(2,1)S(1)} %conv_grads.1), channel_id=1, replica_groups=mesh['seq'=8,'chan'=4] {'seq','chan'}, dimensions={0} | all-to-all | bytes 786432 | tf_op jit(solution)/shard_map/all_to_all | solution.py:272
  46.5 1.1 %unpack.1 = (bf16[128,1024]{1,0:T(8,128)(2,1)}, f32[8,4096]{1,0:T(8,128)}) custom-call(bf16[32,48,128]{2,1,0:T(8,128)(2,1)S(1)} %all_to_all.11.mixed_ref), custom_call_target="tpu_custom_call" | custom-call | tf_op jit(solution)/shard_map/unpack/pallas_call | solution.py:273
Async XLA Ops:
  2.5 25.1 %copy-start = (bf16[256,1536]{1,0:T(8,128)(2,1)S(1)}, bf16[256,1536]{1,0:T(8,128)(2,1)}, u32[]{:S(2)}) copy-start(bf16[256,1536]{1,0:T(8,128)(2,1)} %constant.5.clone.inverse_ref) | copy-start | bytes 2359300
  2.5 25.0 %copy-start.1 = (bf16[512,512]{1,0:T(8,128)(2,1)S(1)}, bf16[512,512]{1,0:T(8,128)(2,1)}, u32[]{:S(2)}) copy-start(bf16[512,512]{1,0:T(8,128)(2,1)} %constant.4.clone.forward_ref) | copy-start | bytes 1572868

commit v4 on v3

--- a/solution.py
+++ b/solution.py
@@ -121,12 +121,13 @@
 
 
 def swap_blocks(stacks, table):
-    rows = stacks[0][0].shape[0]
-    side = [jnp.concatenate(parts, axis=1) for parts in stacks]
-    moved = dot(jnp.concatenate(side, axis=0), table).astype(BF16)
-    return [
-        [moved[i * rows : (i + 1) * rows, l * LANES : (l + 1) * LANES] for l in range(4)] for i in range(len(stacks))
-    ]
+    moved = dot(jnp.concatenate([jnp.concatenate(parts, axis=1) for parts in stacks], axis=0), table).astype(BF16)
+    results, start = [], 0
+    for parts in stacks:
+        stop = start + parts[0].shape[0]
+        results.append([moved[start:stop, l * LANES : (l + 1) * LANES] for l in range(4)])
+        start = stop
+    return results
 
 
 def split_rows(values):
@@ -143,28 +144,24 @@
     piece = rows // 4
     tiles = range(width_here // LANES)
 
-    def moved_out(cut, stacks):
-        moved = swap_blocks(stacks, table)
+    table = swap_table()
+    for copy in arriving:
+        copy.wait()
+    stacks = []
+    for source in (grad_ref, signal_ref):
+        for tile in tiles:
+            columns = slice(tile * LANES, (tile + 1) * LANES)
+            stacks.append([source[q * piece : (q + 1) * piece, columns] for q in range(4)])
+    for tile in tiles:
+        starts = [c * width_here + tile * LANES for c in range(4)]
+        stacks.append([split_rows(taps_ref[:, start : start + LANES]) for start in starts])
+    moved = swap_blocks(stacks, table)
+    count = len(tiles)
+    cuts = (slice(0, piece), slice(piece, 2 * piece), slice(2 * piece, out_ref.shape[1]))
+    for index, cut in enumerate(cuts):
         for tile in tiles:
             for l in range(4):
-                out_ref[tile * 4 + l, cut, :] = moved[tile][l]
-
-    table = swap_table()
-    for index, source in enumerate((grad_ref, signal_ref)):
-        arriving[index].wait()
-        moved_out(
-            slice(index * piece, (index + 1) * piece),
-            [
-                [source[q * piece : (q + 1) * piece, tile * LANES : (tile + 1) * LANES] for q in range(4)]
-                for tile in tiles
-            ],
-        )
-    arriving[2].wait()
-    starts = [[c * width_here + tile * LANES for c in range(4)] for tile in tiles]
-    moved_out(
-        slice(2 * piece, out_ref.shape[1]),
-        [[split_rows(taps_ref[:, at : at + LANES]) for at in row] for row in starts],
-    )
+                out_ref[tile * 4 + l, cut, :] = moved[index * count + tile][l]
 
 
 def lane_limit(supports, width):
@@ -191,15 +188,13 @@
     per_block = lags // (4 * piece)
     table = swap_table()
 
-    def gathered(at):
-        moved = swap_blocks(
-            [[mixed_ref[s * 4 + c, at : at + piece, :] for c in range(4)] for s in range(seq_count)], table
-        )
-        flat = [part for parts in moved for part in parts]
-        size = 4 * per_block
-        return [jnp.concatenate(flat[k : k + size], axis=0) for k in range(0, len(flat), size)]
-
-    upstream, signal = gathered(0), gathered(piece)
+    stacks = [
+        [mixed_ref[s * 4 + c, at : at + piece, :] for c in range(4)] for at in (0, piece) for s in range(seq_count)
+    ]
+    flat = [part for parts in swap_blocks(stacks, table) for part in parts]
+    size = 4 * per_block
+    joined = [jnp.concatenate(flat[k : k + size], axis=0) for k in range(0, len(flat), size)]
+    upstream, signal = joined[: len(joined) // 2], joined[len(joined) // 2 :]
     tap_parts = mixed_ref[:, 2 * piece :, :].astype(F32)
     groups_here = support_ref.shape[0] // 4
     index = lax.axis_index("seq")
@@ -226,16 +221,16 @@
     own = filter_ref.shape[0]
     tiles = range(width_here // LANES)
     table = swap_table()
-    moved = swap_blocks([[mixed_ref[tile * 4 + l, 0:piece, :] for l in range(4)] for tile in tiles], table)
+    cuts = (slice(0, piece), slice(piece, mixed_ref.shape[1]))
+    moved = swap_blocks([[mixed_ref[tile * 4 + l, cut, :] for l in range(4)] for cut in cuts for tile in tiles], table)
     for tile in tiles:
         for q in range(4):
             out_ref[q * piece : (q + 1) * piece, tile * LANES : (tile + 1) * LANES] = moved[tile][q]
     first = pltpu.make_async_copy(out_ref, out_hbm, sems.at[0])
     first.start()
-    moved = swap_blocks([[mixed_ref[tile * 4 + l, piece:, :] for l in range(4)] for tile in tiles], table)
     for tile in tiles:
         for c in range(4):
-            both = moved[tile][c].astype(F32)
+            both = moved[len(tiles) + tile][c].astype(F32)
             start = c * width_here + tile * LANES
             filter_ref[:, start : start + LANES] = both[:own] + both[own:]
     second = pltpu.make_async_copy(filter_ref, filter_hbm, sems.at[1])

time: 47.8 us -> 47.6 us (level)
  no operation moved by 1% of the time
where the time goes in v4:
time: 47.6 us; the launch traced here: 47.4 us
  blocking collectives  41.5 us (87%)
  Pallas kernels  5.22 us (11%)
  between operations  0.66 us (1%)
    all_to_all x2, blocking collectives, fast_body(): lax.all_to_all(mixed, EVERY, split_axis=0, concat_axis=0, tiled=True)  41.5 us
    pallas_call x1, Pallas kernels, fast_body(): pl.pallas_call(functools.partial(fast_kernel, lags, piece), out_shape=jax...  2.49 us
    pallas_call x1, Pallas kernels, fast_body(): pl.pallas_call(pack_kernel, out_shape=pltpu.VMEM((devices, 2 * piece + 2...  1.59 us
    pallas_call x1, Pallas kernels, fast_body(): pl.pallas_call(unpack_kernel, out_shape=(jax.ShapeDtypeStruct((block_len,...  1.14 us

profile of v4, /device:TPU:0, one launch (start us, length us, event | category | flops | bytes accessed | tf_op | source)
XLA Modules:
  0.0 47.4 jit_solution(11655026361894605553)
XLA Ops:
  0.6 1.6 %pack.1 = bf16[32,80,128]{2,1,0:T(8,128)(2,1)S(1)} custom-call(bf16[128,1024]{1,0:T(8,128)(2,1)} %grad_hbm.1, bf16[128,1024]{1,0:T(8,128)(2,1)} %signal_hbm.1, f32[8,4096]{1,0:T(8,128)} %taps_hbm.1), custom_call_target="tpu_custom_call" | custom-call | tf_op jit(solution)/shard_map/pack/pallas_call | solution.py:249
  2.2 0.0 copy-start
  2.2 0.0 copy-start.1
  2.3 25.0 %all_to_all.10.mixed_ref = bf16[32,80,128]{2,1,0:T(8,128)(2,1)S(1)} all-to-all(bf16[32,80,128]{2,1,0:T(8,128)(2,1)S(1)} %pack.1), channel_id=1, replica_groups=mesh['seq'=8,'chan'=4] {'seq','chan'}, dimensions={0} | all-to-all | bytes 1310720 | tf_op jit(solution)/shard_map/all_to_all | solution.py:259
  27.3 0.0 copy-done
  27.3 0.0 copy-done.1
  27.3 2.5 %conv_grads.1 = bf16[32,48,128]{2,1,0:T(8,128)(2,1)S(1)} custom-call(s32[32]{0:T(128)} %support_hbm.1, bf16[32,80,128]{2,1,0:T(8,128)(2,1)S(1)} %all_to_all.10.mixed_ref, bf16[512,512]{1,0:T(8,128)(2,1)S(1)} %copy-done.1, bf16[256,1536]{1,0:T(8,128)(2,1)S(1)} %copy-done), custom_call_target="tpu_custom_call" | custom-call | tf_op jit(solution)/shard_map/conv_grads/pallas_call | solution.py:260
  29.8 16.5 %all_to_all.11.mixed_ref = bf16[32,48,128]{2,1,0:T(8,128)(2,1)S(1)} all-to-all(bf16[32,48,128]{2,1,0:T(8,128)(2,1)S(1)} %conv_grads.1), channel_id=1, replica_groups=mesh['seq'=8,'chan'=4] {'seq','chan'}, dimensions={0} | all-to-all | bytes 786432 | tf_op jit(solution)/shard_map/all_to_all | solution.py:267
  46.3 1.1 %unpack.1 = (bf16[128,1024]{1,0:T(8,128)(2,1)}, f32[8,4096]{1,0:T(8,128)}) custom-call(bf16[32,48,128]{2,1,0:T(8,128)(2,1)S(1)} %all_to_all.11.mixed_ref), custom_call_target="tpu_custom_call" | custom-call | tf_op jit(solution)/shard_map/unpack/pallas_call | solution.py:268
Async XLA Ops:
  2.2 25.0 %copy-start = (bf16[256,1536]{1,0:T(8,128)(2,1)S(1)}, bf16[256,1536]{1,0:T(8,128)(2,1)}, u32[]{:S(2)}) copy-start(bf16[256,1536]{1,0:T(8,128)(2,1)} %constant.5.clone.inverse_ref) | copy-start | bytes 2359300
  2.2 25.0 %copy-start.1 = (bf16[512,512]{1,0:T(8,128)(2,1)S(1)}, bf16[512,512]{1,0:T(8,128)(2,1)}, u32[]{:S(2)}) copy-start(bf16[512,512]{1,0:T(8,128)(2,1)} %constant.4.clone.forward_ref) | copy-start | bytes 1572868
